TPU v7x, 32 devices: a whole 2x2x4 slice. The times are simulated.
32 devices in a mesh: groups: 2 (over y), feat: 4 (over z), dp: 4 (over x, core).
Axes of the slice: x: 2, y: 2, z: 4, core: 2. Of those that a mesh axis runs over, the one named last changes fastest.
Arguments:
- activations: bfloat16 [12288, 29568], P(('groups', 'dp'), 'feat'), parts along dimension 0, may hold values from -6 to 6
- test_matrix: bfloat16 [29568, 512], P('feat'), may hold values from -6 to 6
Outputs:
- range_sketch: float32 [1024, 29568], P(('groups', 'dp'), 'feat'), parts along dimension 0
- core: float32 [1024, 512], P(('groups', 'dp')), parts along dimension 0
There are 2 independent parts, one for each index of `groups`. A program takes and returns all parts, laid end to end along the dimension named above; an argument that names none is the same for every part. Nothing has to cross between parts.
All inputs are finite; a program needn't handle non-finite values.
Results may differ from a plain program's by a relative error of at most 0.0026.
Values may be sent and summed in bfloat16 or wider, within the bound.
A program may use at most 128 MiB of HBM per device.

v0:
```python
import jax
import jax.numpy as jnp
from jax import lax
from jax.sharding import PartitionSpec as P

F = 29568


def body(activations, test_matrix):
    tokens_here = activations.shape[0]
    inverse_tokens = 1.0 / (tokens_here * lax.axis_size("dp"))
    partial_rows = jnp.dot(activations, test_matrix, preferred_element_type=jnp.float32)
    shares = lax.psum_scatter(partial_rows, "feat", scatter_dimension=1, tiled=True).astype(
        jnp.bfloat16
    )
    sketched = lax.all_gather(shares, "feat", axis=1, tiled=True)
    product = lax.dot_general(
        sketched, activations, (((0,), (0,)), ((), ())), preferred_element_type=jnp.float32
    )
    range_sketch = lax.psum_scatter(product * inverse_tokens, "dp", scatter_dimension=0, tiled=True)
    core_part = jnp.dot(
        range_sketch, test_matrix.astype(jnp.float32), precision=lax.Precision.HIGHEST
    ) * (1.0 / F)
    core = lax.psum(core_part, "feat")
    return (range_sketch, core)


def solution(mesh):
    placed = (P(("groups", "dp"), "feat"), P("feat", None))
    return jax.shard_map(
        body,
        mesh=mesh,
        in_specs=placed,
        out_specs=(P(("groups", "dp"), "feat"), P(("groups", "dp"), None)),
        check_vma=False,
    )
```

profile of v0, /device:TPU:0, one launch (start us, length us, event | category | flops | bytes accessed | tf_op | source)
XLA Modules:
  0.0 315.7 jit_solution(10915818249523577421)
XLA Ops:
  7.2 0.0 reduce-scatter.3.cloned.1.call-start
  7.2 18.6 %fusion = f32[1536,512]{1,0:T(8,128)} fusion(bf16[1536,7392]{0,1:T(8,128)(2,1)} %param.2, bf16[7392,512]{1,0:T(8,128)(2,1)} %param.3), kind=kOutput, calls=%fused_computation.2 | convolution fusion | flops 11626610688 | bytes 33423360 | tf_op jit(solution)/shard_map/dot_general | solution.py:12
  25.8 0.0 reduce-scatter.3.cloned.1.call-update
  25.9 0.0 all-gather.2.cloned.1.call-start
  25.9 63.1 %reduce-scatter.3.cloned.1.call-done = f32[1536,128]{1,0:T(8,128)} async-done(((f32[1536,512]{1,0:T(8,128)}), f32[1536,128]{1,0:T(8,128)}) %reduce-scatter.3.cloned.1.call-update) | async-done | bytes 786448 | tf_op jit(solution)/shard_map/reduce_scatter | solution.py:13
  89.0 1.9 convert_element_type.4
  90.9 0.0 all-gather.2.cloned.1.call-update
  90.9 0.0 reduce-scatter.5.cloned.1.call-start
  91.0 37.9 %all-gather.2.cloned.1.call-done = bf16[1536,512]{1,0:T(8,128)(2,1)} async-done(((bf16[1536,128]{1,0:T(8,128)(2,1)}), bf16[1536,512]{1,0:T(8,128)(2,1)}) %all-gather.2.cloned.1.call-update) | async-done | bytes 1572880 | tf_op jit(solution)/shard_map/all_gather | solution.py:16
  128.9 19.9 %convolution_multiply_fusion = f32[512,7392]{0,1:T(8,128)} fusion(bf16[1536,7392]{0,1:T(8,128)(2,1)} %param.2, bf16[1536,512]{1,0:T(8,128)(2,1)} %all-gather.2.cloned.1.call-done), kind=kOutput, calls=%fused_computation | convolution fusion | flops 11630395392 | bytes 39419904 | tf_op jit(solution)/shard_map/dot_general | solution.py:17
  148.7 0.0 reduce-scatter.5.cloned.1.call-update
  148.8 0.2 all-reduce.2.cloned.1.call-start
  149.0 114.1 %reduce-scatter.5.cloned.1.call-done = f32[128,7392]{0,1:T(8,128)} async-done(((f32[512,7392]{0,1:T(8,128)}), f32[128,7392]{0,1:T(8,128)}) %reduce-scatter.5.cloned.1.call-update) | async-done | bytes 3784720 | tf_op jit(solution)/shard_map/reduce_scatter | solution.py:20
  263.1 8.8 %convolution_multiply_fusion.1 = f32[128,512]{1,0:T(8,128)} fusion(f32[128,7392]{0,1:T(8,128)} %reduce-scatter.5.cloned.1.call-done, bf16[7392,512]{1,0:T(8,128)(2,1)} %param.3), kind=kOutput, calls=%fused_computation.1 | convolution fusion | flops 5813370880 | bytes 11616256 | tf_op jit(solution)/shard_map/dot_general | solution.py:21
  272.0 0.0 all-reduce.2.cloned.1.call-update
  272.0 35.5 %all-reduce.2.cloned.1.call-done = f32[128,512]{1,0:T(8,128)} async-done(((f32[128,512]{1,0:T(8,128)}), f32[128,512]{1,0:T(8,128)}) %all-reduce.2.cloned.1.call-update) | async-done | bytes 262160 | tf_op jit(solution)/shard_map/psum | solution.py:24
  307.5 1.7 copy.5
Async XLA Ops:
  7.2 81.8 %reduce-scatter.3.cloned.1.call-start = ((), (), s32[]{:S(2)}) async-start(), calls=%async_computation.2 | async-start | bytes 3932160 | tf_op jit(solution)/shard_map/reduce_scatter | solution.py:13
  25.9 103.0 %all-gather.2.cloned.1.call-start = ((), (), s32[]{:S(2)}) async-start(), calls=%async_computation.3 | async-start | bytes 1966080 | tf_op jit(solution)/shard_map/all_gather | solution.py:16
  90.9 172.2 %reduce-scatter.5.cloned.1.call-start = ((), (), s32[]{:S(2)}) async-start(), calls=%async_computation.4 | async-start | bytes 18923520 | tf_op jit(solution)/shard_map/reduce_scatter | solution.py:20
  148.8 158.7 %all-reduce.2.cloned.1.call-start = ((), (), s32[]{:S(2)}) async-start(), calls=%async_computation.5 | async-start | bytes 524288 | tf_op jit(solution)/shard_map/psum | solution.py:24
Sparse Core Ops, SparseCore 0:
  26.0 62.9 reduce-scatter.2
  91.1 37.7 all-gather.1
  148.9 114.1 reduce-scatter.4
  272.1 35.3 all-reduce.1
where the time goes:
time: 316 us
  waiting for transfers between devices  251 us (79%)
  matrix products  47.3 us (15%)
  between operations  13.8 us (4%)
    reduce_scatter x1, waiting for transfers between devices, body(): lax.psum_scatter(product * inverse_tokens, 'dp', scatter_dimension=0, til...  114 us
    reduce_scatter x1, waiting for transfers between devices, body(): lax.psum_scatter(partial_rows, 'feat', scatter_dimension=1, tiled=True)  63.1 us
    all_gather x1, waiting for transfers between devices, body(): sketched = lax.all_gather(shares, 'feat', axis=1, tiled=True)  37.9 us
    psum x1, waiting for transfers between devices, body(): core = lax.psum(core_part, 'feat')  35.5 us
    dot_general x1, matrix products, body(): lax.dot_general(sketched, activations, (((0,), (0,)), ((), ())), preferre...  19.9 us
    dot_general x1, matrix products, body(): jnp.dot(activations, test_matrix, preferred_element_type=jnp.float32)  18.6 us
    dot_general x1, matrix products, body(): jnp.dot(range_sketch, test_matrix.astype(jnp.float32), precision=lax.Prec...  8.85 us
  transfers between devices with their start and end apart: 4, of which 4 were waited for; matrix products, arithmetic and copies ran while one was open for 0% of the time, Pallas kernels for 0%

commit v1 on v0

v1 whole, which is shorter than its diff:
```python
import functools

import jax
import jax.numpy as jnp
from jax import lax
from jax.experimental import pallas as pl
from jax.experimental.pallas import tpu as pltpu
from jax.sharding import PartitionSpec as P

F = 29568
MESH = pl.DeviceIdType.MESH
F32, BF16 = jnp.float32, jnp.bfloat16
TB = 256
CB = 512


def plain(activations, test_matrix):
    tokens_here = activations.shape[0]
    inverse_tokens = 1.0 / (tokens_here * lax.axis_size("dp"))
    partial_rows = jnp.dot(activations, test_matrix, preferred_element_type=F32)
    shares = lax.psum_scatter(partial_rows, "feat", scatter_dimension=1, tiled=True).astype(BF16)
    sketched = lax.all_gather(shares, "feat", axis=1, tiled=True)
    product = lax.dot_general(
        sketched, activations, (((0,), (0,)), ((), ())), preferred_element_type=F32
    )
    range_sketch = lax.psum_scatter(product * inverse_tokens, "dp", scatter_dimension=0, tiled=True)
    core_part = jnp.dot(
        range_sketch, test_matrix.astype(F32), precision=lax.Precision.HIGHEST
    ) * (1.0 / F)
    core = lax.psum(core_part, "feat")
    return (range_sketch, core)


def kernel(
    inv_t, inv_core,
    a_hbm, om_hbm, range_ref, core_ref,
    a, om1, om2, st, p1, p2, z1s, z1p, z1t, z2p, z2t,
    ps, pr, qs, qr, keep, xs, xr,
    cpart, cpr, cxs, cxr, cout,
    ld, zs, zr, zs2, zr2, ss, sr, psem, prem, qsem, qrem, xsem, xrem, csem, crem,
):
    T, W = a.shape
    NB = T // TB
    FULL = W // CB
    TAIL = W - FULL * CB
    TAILP = -(-TAIL // 128) * 128

    z = lax.axis_index("feat")
    d = lax.axis_index("dp")
    x, c = d // 2, d % 2
    inner = jnp.logical_and(z >= 1, z <= 2)
    outer = jnp.logical_not(inner)
    hop = jnp.where(inner, 3 * (z - 1), 1 + z // 3)
    hop = jnp.clip(hop, 0, 3)
    mid = jnp.clip(3 - z, 0, 3)
    pair = 2 * x + (1 - c)
    across = 2 * (1 - x) + c

    def rows(ref, s):
        return ref.at[pl.ds(pl.multiple_of(s * TB, TB), TB), :]

    h_other = pl.multiple_of((1 - x) * 256, 256)
    h_own = pl.multiple_of(x * 256, 256)

    ld_om1 = pltpu.make_async_copy(om_hbm.at[:, pl.ds(h_other, 256)], om1, ld.at[NB])
    ld_om2 = pltpu.make_async_copy(om_hbm.at[:, pl.ds(h_own, 256)], om2, ld.at[NB + 1])

    def ld_a(s):
        return pltpu.make_async_copy(rows(a_hbm, s), rows(a, s), ld.at[s])

    ld_om1.start()
    ld_a(0).start()
    ld_om2.start()
    for s in range(1, NB):
        ld_a(s).start()

    barrier = pltpu.get_barrier_semaphore()
    for k in range(1, 4):
        pl.semaphore_signal(barrier, inc=1, device_id={"feat": lax.rem(z + k, 4)}, device_id_type=MESH)
    for other in (pair, across):
        pl.semaphore_signal(barrier, inc=1, device_id={"dp": other}, device_id_type=MESH)
    pl.semaphore_wait(barrier, 5)

    def rcopy(src, dst, s1, s2, dev):
        return pltpu.make_async_remote_copy(
            src_ref=src, dst_ref=dst, send_sem=s1, recv_sem=s2, device_id=dev, device_id_type=MESH
        )

    def first_p(s):
        return rcopy(rows(z1s, s), rows(z1p, s), zs.at[0, s], zr.at[0, s], {"feat": hop})

    def first_t(s):
        return rcopy(rows(z1s, s), rows(z1t, s), zs.at[1, s], zr.at[1, s], {"feat": mid})

    def second_p(s):
        return rcopy(rows(p2, s), rows(z2p, s), zs2.at[0, s], zr2.at[0, s], {"feat": hop})

    def second_t(s):
        return rcopy(rows(p2, s), rows(z2t, s), zs2.at[1, s], zr2.at[1, s], {"feat": mid})

    def st_at(h, s):
        return st.at[pl.ds(h, 256), pl.ds(pl.multiple_of(s * TB, TB), TB)]

    def send_s(half, h, s):
        return rcopy(st_at(h, s), st_at(h, s), ss.at[half, s], sr.at[half, s], {"feat": hop})

    ld_om1.wait()

    @pl.loop(0, NB + 2)
    def _(s):
        @pl.when(s < NB)
        def _():
            ld_a(s).wait()
            part = jnp.dot(rows(a, s)[...], om1[...], preferred_element_type=F32)

            @pl.when(outer)
            def _():
                rows(z1s, s)[...] = part.astype(BF16)
                first_p(s).start()

            @pl.when(inner)
            def _():
                rows(p1, s)[...] = part

        @pl.when(jnp.logical_and(inner, jnp.logical_and(s >= 1, s <= NB)))
        def _():
            k = s - 1
            first_p(k).wait_recv()
            total = rows(p1, k)[...] + rows(z1p, k)[...].astype(F32)
            rows(p1, k)[...] = total
            rows(z1s, k)[...] = total.astype(BF16)
            first_t(k).start()

        @pl.when(s == 0)
        def _():
            ld_om2.wait()

        @pl.when(s < NB)
        def _():
            rows(p2, s)[...] = jnp.dot(rows(a, s)[...], om2[...], preferred_element_type=F32)

        @pl.when(jnp.logical_and(inner, s >= 2))
        def _():
            k = s - 2
            first_t(k).wait_recv()
            total = rows(p1, k)[...] + rows(z1t, k)[...].astype(F32)
            st_at(h_other, k)[...] = total.T.astype(BF16)
            send_s(0, h_other, k).start()

    @pl.when(outer)
    def _():
        @pl.loop(0, NB)
        def _(s):
            second_p(s).start()

        @pl.loop(0, NB)
        def _(s):
            send_s(0, h_other, s).wait_recv()

    if TAIL:
        for buf in (ps, qs, xs):
            buf[FULL] = jnp.zeros(buf.shape[1:], BF16)

    def span(j, width):
        return pl.ds(j * CB, width) if isinstance(j, int) else pl.ds(pl.multiple_of(j * CB, CB), width)

    def pcopy(j, wp):
        view = lambda r: r.at[j, :, pl.ds(0, wp)]
        return rcopy(view(ps), view(pr), psem.at[j], prem.at[j], {"dp": pair})

    def qcopy(j, wp):
        view = lambda r: r.at[j, :, pl.ds(0, wp)]
        return rcopy(view(qs), view(qr), qsem.at[j], qrem.at[j], {"dp": pair})

    def xcopy(j, wp):
        view = lambda r: r.at[j, :, pl.ds(0, wp)]
        return rcopy(view(xs), view(xr), xsem.at[j], xrem.at[j], {"dp": across})

    mine = pl.multiple_of(c * 128, 128)
    theirs = pl.multiple_of((1 - c) * 128, 128)

    def product(h, base, j, width):
        return jnp.dot(st[pl.ds(h + base, 128), :], a[:, span(j, width)], preferred_element_type=F32)

    def multiply(h, j, width, wp, out, copy):
        out[j, :, pl.ds(0, width)] = product(h, theirs, j, width).astype(BF16)
        copy(j, wp).start()
        keep[lax.rem(j, 2), :, pl.ds(0, width)] = product(h, mine, j, width)

    def combine_x(j, width, wp):
        pcopy(j, wp).wait_recv()
        total = keep[lax.rem(j, 2), :, pl.ds(0, width)] + pr[j, :, pl.ds(0, width)].astype(F32)
        xs[j, :, pl.ds(0, width)] = total.astype(BF16)
        xcopy(j, wp).start()

    def combine_out(j, width, wp):
        qcopy(j, wp).wait_recv()
        xcopy(j, wp).wait_recv()
        total = keep[lax.rem(j, 2), :, pl.ds(0, width)] + qr[j, :, pl.ds(0, width)].astype(F32)
        total = total + xr[j, :, pl.ds(0, width)].astype(F32)
        range_ref[:, span(j, width)] = total * inv_t

    def sweep(h, out, copy, combine):
        multiply(h, 0, CB, CB, out, copy)

        @pl.loop(1, FULL)
        def _(j):
            multiply(h, j, CB, CB, out, copy)
            combine(j - 1, CB, CB)

        if TAIL:
            multiply(h, FULL, TAIL, TAILP, out, copy)
        combine(FULL - 1, CB, CB)
        if TAIL:
            combine(FULL, TAIL, TAILP)

    sweep(h_other, ps, pcopy, combine_x)

    @pl.when(inner)
    def _():
        @pl.loop(0, NB + 1)
        def _(s):
            @pl.when(s < NB)
            def _():
                second_p(s).wait_recv()
                rows(p2, s)[...] = rows(p2, s)[...] + rows(z2p, s)[...]
                second_t(s).start()

            @pl.when(s >= 1)
            def _():
                k = s - 1
                second_t(k).wait_recv()
                total = rows(p2, k)[...] + rows(z2t, k)[...]
                st_at(h_own, k)[...] = total.T.astype(BF16)
                send_s(1, h_own, k).start()

    @pl.when(outer)
    def _():
        @pl.loop(0, NB)
        def _(s):
            send_s(1, h_own, s).wait_recv()

    cols = st[pl.ds(pl.multiple_of(z * 128, 128), 128), :]
    for q in range(4):
        cpart[q] = lax.dot_general(
            st[pl.ds(q * 128, 128), :], cols, (((1,), (1,)), ((), ())), preferred_element_type=F32
        )

    def cpair(k):
        owner = 2 * ((1 - x) if k == 0 else x)
        return rcopy(cpart.at[owner + 1 - c], cpr.at[k], csem.at[k], crem.at[k], {"dp": pair})

    cpair(0).start()
    cpair(1).start()
    cross = rcopy(cxs, cxr, csem.at[2], crem.at[2], {"dp": across})
    cpair(0).wait_recv()
    cxs[...] = cpart[2 * (1 - x) + c] + cpr[0]
    cross.start()

    def ccopy(k):
        return rcopy(cout.at[0], cout.at[k], csem.at[2 + k], crem.at[2 + k], {"feat": lax.rem(z + k, 4)})

    def finish_core():
        cpair(1).wait_recv()
        cross.wait_recv()
        cout[0] = (cpart[2 * x + c] + cpr[1] + cxr[...]) * inv_core
        for k in range(1, 4):
            ccopy(k).start()

    finish_core()
    sweep(h_own, qs, qcopy, combine_out)

    for k in range(1, 4):
        ccopy(k).wait_recv()
    for k in range(4):
        at = pl.multiple_of(lax.rem(z - k + 4, 4) * 128, 128)
        core_ref[:, pl.ds(at, 128)] = cout[k]

    cpair(0).wait_send()
    cpair(1).wait_send()
    cross.wait_send()
    for k in range(1, 4):
        ccopy(k).wait_send()

    @pl.loop(0, NB)
    def _(s):
        @pl.when(outer)
        def _():
            first_p(s).wait_send()
            second_p(s).wait_send()

        @pl.when(inner)
        def _():
            first_t(s).wait_send()
            second_t(s).wait_send()
            send_s(0, h_other, s).wait_send()
            send_s(1, h_own, s).wait_send()

    def drain(j, wp):
        pcopy(j, wp).wait_send()
        qcopy(j, wp).wait_send()
        xcopy(j, wp).wait_send()

    @pl.loop(0, FULL)
    def _(j):
        drain(j, CB)

    if TAIL:
        drain(FULL, TAILP)


def fused(activations, test_matrix):
    T, W = activations.shape
    R = test_matrix.shape[1]
    NB = T // TB
    NC = -(-W // CB)
    tokens = T * lax.axis_size("dp")
    units = W * lax.axis_size("feat")
    DMA = pltpu.SemaphoreType.DMA
    V = pltpu.VMEM
    return pl.pallas_call(
        functools.partial(kernel, 1.0 / tokens, 1.0 / tokens / units),
        out_shape=(
            jax.ShapeDtypeStruct((R // 4, W), F32),
            jax.ShapeDtypeStruct((R // 4, R), F32),
        ),
        in_specs=[pl.BlockSpec(memory_space=pl.ANY)] * 2,
        out_specs=(pl.BlockSpec(memory_space=pltpu.VMEM),) * 2,
        scratch_shapes=[
            V((T, W), BF16), V((W, 256), BF16), V((W, 256), BF16), V((R, T), BF16),
            V((T, 256), F32), V((T, 256), F32),
            V((T, 256), BF16), V((T, 256), BF16), V((T, 256), BF16),
            V((T, 256), F32), V((T, 256), F32),
            V((NC, 128, CB), BF16), V((NC, 128, CB), BF16), V((NC, 128, CB), BF16), V((NC, 128, CB), BF16),
            V((2, 128, CB), F32),
            V((NC, 128, CB), BF16), V((NC, 128, CB), BF16),
            V((4, 128, 128), F32), V((2, 128, 128), F32), V((128, 128), F32), V((128, 128), F32),
            V((4, 128, 128), F32),
            DMA((NB + 2,)), DMA((2, NB)), DMA((2, NB)), DMA((2, NB)), DMA((2, NB)), DMA((2, NB)), DMA((2, NB)),
            DMA((NC,)), DMA((NC,)), DMA((NC,)), DMA((NC,)), DMA((NC,)), DMA((NC,)),
            DMA((6,)), DMA((6,)),
        ],
        compiler_params=pltpu.CompilerParams(
            collective_id=0, has_side_effects=True, vmem_limit_bytes=63 * 1024 * 1024
        ),
        cost_estimate=pl.CostEstimate(
            flops=4 * T * W * R, bytes_accessed=2 * T * W + 4 * W * R, transcendentals=0
        ),
    )(activations, test_matrix)


def solution(mesh):
    placed = (P(("groups", "dp"), "feat"), P("feat", None))

    def body(activations, test_matrix):
        T, W = activations.shape
        fits = (
            mesh.shape["feat"] == 4
            and mesh.shape["dp"] == 4
            and test_matrix.shape[1] == 512
            and T % TB == 0
            and W % 16 == 0
            and 2 * CB <= W <= 7424
            and T <= 1536
        )
        return (fused if fits else plain)(activations, test_matrix)

    return jax.shard_map(
        body,
        mesh=mesh,
        in_specs=placed,
        out_specs=(P(("groups", "dp"), "feat"), P(("groups", "dp"), None)),
        check_vma=False,
    )
```

time: 316 us -> 139 us (0.44)
  waiting for transfers between devices: 251 us -> 0 us
  Pallas kernels: 0 us -> 104 us
  matrix products: 47.3 us -> 0 us
  local copies, waits for them, and re-layouts: 1.67 us -> 33.2 us
  between operations: 13.8 us -> 0.65 us
    reduce_scatter x2 -> x0, waiting for transfers between devices: 177 us -> none  [the longest x1 114 us: body(): lax.psum_scatter(product * inverse_tokens, 'dp', scatter_dimension=0, til...]
    pallas_call x0 -> x1, Pallas kernels: none -> 104 us  [fused(): pl.pallas_call(functools.partial(kernel, 1.0 / tokens, 1.0 / tokens / uni...]
    dot_general x3 -> x0, matrix products: 47.3 us -> none  [the longest x1 19.9 us: body(): lax.dot_general(sketched, activations, (((0,), (0,)), ((), ())), preferre...]
    all_gather x1 -> x0, waiting for transfers between devices: 37.9 us -> none  [body(): sketched = lax.all_gather(shares, 'feat', axis=1, tiled=True)]
    psum x1 -> x0, waiting for transfers between devices: 35.5 us -> none  [body(): core = lax.psum(core_part, 'feat')]
    unnamed x1 -> x4, local copies, waits for them, and re-layouts: 1.67 us -> 27.9 us
    pallas_call x0 -> x1, local copies, waits for them, and re-layouts: none -> 5.31 us  [fused(): pl.pallas_call(functools.partial(kernel, 1.0 / tokens, 1.0 / tokens / uni...]
  transfers between devices with their start and end apart: 4 -> 0, of which waited for: 4 -> 0; matrix products, arithmetic and copies ran while one was open for 0% -> 0% of each run, Pallas kernels for 0% -> 0%
where the time goes in v1:
time: 139 us; the launch traced here: 138 us
  Pallas kernels  104 us (75%)
  local copies, waits for them, and re-layouts  33.2 us (24%)
    pallas_call x1, Pallas kernels, fused(): pl.pallas_call(functools.partial(kernel, 1.0 / tokens, 1.0 / tokens / uni...  104 us
    unnamed x4, local copies, waits for them, and re-layouts  27.9 us
    pallas_call x1, local copies, waits for them, and re-layouts, fused(): pl.pallas_call(functools.partial(kernel, 1.0 / tokens, 1.0 / tokens / uni...  5.31 us

profile of v1, /device:TPU:0, one launch (start us, length us, event | category | flops | bytes accessed | tf_op | source)
XLA Modules:
  0.0 138.2 jit_solution(15811319738454622831)
XLA Ops:
  0.6 27.2 %copy.4.a_hbm = bf16[1536,7392]{1,0:T(8,128)(2,1)} copy(bf16[1536,7392]{0,1:T(8,128)(2,1)} %param.2) | data formatting | bytes 45416448 | tf_op args[0]
  27.9 104.3 %shard_map.41 = (f32[128,7392]{1,0:T(8,128)}, f32[128,512]{1,0:T(8,128)}) custom-call(bf16[1536,7392]{1,0:T(8,128)(2,1)} %copy.4.a_hbm, bf16[7392,512]{1,0:T(8,128)(2,1)} %om_hbm.1), custom_call_target="tpu_custom_call" | custom-call | flops 23253221376 | bytes 37847040 | tf_op jit(solution)/shard_map/pallas_call | solution.py:321
  132.2 0.0 copy-start
  132.2 5.3 %copy.5 = f32[128,7392]{0,1:T(8,128)} copy(f32[128,7392]{1,0:T(8,128)} %get-tuple-element.2) | data formatting | bytes 7569408 | tf_op jit(solution)/shard_map/pallas_call | solution.py:321
  137.5 0.0 copy-done
  137.5 0.7 copy.7
Async XLA Ops:
  132.2 5.3 %copy-start = (f32[128,512]{1,0:T(8,128)S(1)}, f32[128,512]{1,0:T(8,128)}, u32[]{:S(2)}) copy-start(f32[128,512]{1,0:T(8,128)} %get-tuple-element.7) | copy-start | bytes 786436

commit v2 on v0

v2 whole, which is shorter than its diff:
```python
import functools

import jax
import jax.numpy as jnp
from jax import lax
from jax.experimental import pallas as pl
from jax.experimental.pallas import tpu as pltpu
from jax.sharding import PartitionSpec as P

F = 29568
MESH = pl.DeviceIdType.MESH
F32, BF16 = jnp.float32, jnp.bfloat16
TB = 256
CB = 512


def plain(activations, test_matrix):
    tokens_here = activations.shape[0]
    inverse_tokens = 1.0 / (tokens_here * lax.axis_size("dp"))
    partial_rows = jnp.dot(activations, test_matrix, preferred_element_type=F32)
    shares = lax.psum_scatter(partial_rows, "feat", scatter_dimension=1, tiled=True).astype(BF16)
    sketched = lax.all_gather(shares, "feat", axis=1, tiled=True)
    product = lax.dot_general(
        sketched, activations, (((0,), (0,)), ((), ())), preferred_element_type=F32
    )
    range_sketch = lax.psum_scatter(product * inverse_tokens, "dp", scatter_dimension=0, tiled=True)
    core_part = jnp.dot(
        range_sketch, test_matrix.astype(F32), precision=lax.Precision.HIGHEST
    ) * (1.0 / F)
    core = lax.psum(core_part, "feat")
    return (range_sketch, core)


def kernel(
    inv_core,
    a_hbm, om_hbm, range_ref, core_ref,
    a, om, omt, st, p1, p2, z1s, z1p, z1t, z2p, z2t,
    ps, pr, qs, qr, keep, xs, xr,
    cpart, cpr, cxs, cxr, cout,
    ld, lo, zs, zr, zs2, zr2, ss, sr, psem, prem, qsem, qrem, xsem, xrem, csem, crem,
):
    W, T = a.shape
    NB = T // TB
    FULL = W // CB
    TAIL = W - FULL * CB

    z = lax.axis_index("feat")
    d = lax.axis_index("dp")
    x, c = d // 2, d % 2
    inner = jnp.logical_and(z >= 1, z <= 2)
    outer = jnp.logical_not(inner)
    hop = jnp.where(inner, 3 * (z - 1), 1 + z // 3)
    hop = jnp.clip(hop, 0, 3)
    mid = jnp.clip(3 - z, 0, 3)
    pair = 2 * x + (1 - c)
    across = 2 * (1 - x) + c

    def ld_om(half):
        chip = (1 - x) if half == 0 else x
        return [
            pltpu.make_async_copy(
                om_hbm.at[:, pl.ds(pl.multiple_of((2 * chip + core) * 128, 128), 128)],
                om.at[:, pl.ds(at, 128)],
                lo.at[half, at // 128],
            )
            for at, core in ((0, c), (128, 1 - c))
        ]

    def lanes(ref, s):
        return ref.at[:, pl.ds(pl.multiple_of(s * TB, TB), TB)]

    def ld_a(s):
        return pltpu.make_async_copy(lanes(a_hbm, s), lanes(a, s), ld.at[s])

    for copy in ld_om(0):
        copy.start()
    for s in range(2):
        ld_a(s).start()

    barrier = pltpu.get_barrier_semaphore()
    for k in range(1, 4):
        pl.semaphore_signal(barrier, inc=1, device_id={"feat": lax.rem(z + k, 4)}, device_id_type=MESH)
    for other in (pair, across):
        pl.semaphore_signal(barrier, inc=1, device_id={"dp": other}, device_id_type=MESH)
    pl.semaphore_wait(barrier, 5)

    def rcopy(src, dst, s1, s2, dev):
        return pltpu.make_async_remote_copy(
            src_ref=src, dst_ref=dst, send_sem=s1, recv_sem=s2, device_id=dev, device_id_type=MESH
        )

    def first_p(s, u):
        view = lambda r: r.at[s, pl.ds(128 * u, 128), :]
        return rcopy(view(z1s), view(z1p), zs.at[0, 2 * s + u], zr.at[0, 2 * s + u], {"feat": hop})

    def first_t(s, u):
        view = lambda r: r.at[s, pl.ds(128 * u, 128), :]
        return rcopy(view(z1s), view(z1t), zs.at[1, 2 * s + u], zr.at[1, 2 * s + u], {"feat": mid})

    def first_s(s, u):
        view = st.at[0, pl.ds(pl.multiple_of(s * TB, TB), TB), pl.ds(128 * u, 128)]
        return rcopy(view, view, ss.at[0, 2 * s + u], sr.at[0, 2 * s + u], {"feat": hop})

    def second_p(k):
        return rcopy(p2.at[k], z2p.at[k], zs2.at[0, k], zr2.at[0, k], {"feat": hop})

    def second_t(k):
        return rcopy(p2.at[k], z2t.at[k], zs2.at[1, k], zr2.at[1, k], {"feat": mid})

    def st_at(k):
        rows = pl.ds(pl.multiple_of(lax.rem(k, NB) * TB, TB), TB)
        return st.at[1, rows, pl.ds(pl.multiple_of(jnp.where(k < NB, 128, 0), 128), 128)]

    def second_s(k):
        return rcopy(st_at(k), st_at(k), ss.at[1, k], sr.at[1, k], {"feat": hop})

    def turn(half):
        for copy in ld_om(half):
            copy.wait()

        @pl.loop(0, W // 256)
        def _(k):
            at = pl.ds(pl.multiple_of(k * 256, 256), 256)
            omt[half, :, at] = om[at, :].T

        done = W // 256 * 256
        if W > done:
            omt[half, :, pl.ds(done, W - done)] = om[pl.ds(done, W - done), :].T

    turn(0)
    for copy in ld_om(1):
        copy.start()

    @pl.loop(0, NB + 2)
    def _(s):
        @pl.when(s < NB)
        def _():
            ld_a(s).wait()

            @pl.when(s + 2 < NB)
            def _():
                ld_a(s + 2).start()

            part = jnp.dot(omt[0], lanes(a, s)[...], preferred_element_type=F32)

            @pl.when(outer)
            def _():
                z1s[s] = part.astype(BF16)
                first_p(s, 0).start()
                first_p(s, 1).start()

            @pl.when(inner)
            def _():
                p1[s] = part

        @pl.when(jnp.logical_and(inner, jnp.logical_and(s >= 1, s <= NB)))
        def _():
            k = s - 1
            for u in range(2):
                ranks = pl.ds(128 * u, 128)
                first_p(k, u).wait_recv()
                total = p1[k, ranks, :] + z1p[k, ranks, :].astype(F32)
                p1[k, ranks, :] = total
                z1s[k, ranks, :] = total.astype(BF16)
                first_t(k, u).start()

        @pl.when(s == 0)
        def _():
            turn(1)

        @pl.when(s < NB)
        def _():
            part = jnp.dot(omt[1], lanes(a, s)[...], preferred_element_type=F32)
            p2[s] = part[128:]
            p2[NB + s] = part[:128]

        @pl.when(jnp.logical_and(inner, s >= 2))
        def _():
            k = s - 2
            for u in range(2):
                ranks = pl.ds(128 * u, 128)
                first_t(k, u).wait_recv()
                total = p1[k, ranks, :] + z1t[k, ranks, :].astype(F32)
                st[0, pl.ds(pl.multiple_of(k * TB, TB), TB), ranks] = total.T.astype(BF16)
                first_s(k, u).start()

    @pl.when(outer)
    def _():
        @pl.loop(0, 2 * NB)
        def _(k):
            second_p(k).start()

        @pl.loop(0, NB)
        def _(s):
            first_s(s, 0).wait_recv()
            first_s(s, 1).wait_recv()

    def span(j, width):
        return pl.ds(j * CB, width) if isinstance(j, int) else pl.ds(pl.multiple_of(j * CB, CB), width)

    def pcopy(j, width):
        view = lambda r: r.at[j, pl.ds(0, width), :]
        return rcopy(view(ps), view(pr), psem.at[j], prem.at[j], {"dp": pair})

    def qcopy(j, width):
        view = lambda r: r.at[j, pl.ds(0, width), :]
        return rcopy(view(qs), view(qr), qsem.at[j], qrem.at[j], {"dp": pair})

    def xcopy(j, width):
        view = lambda r: r.at[j, pl.ds(0, width), :]
        return rcopy(view(xs), view(xr), xsem.at[j], xrem.at[j], {"dp": across})

    def multiply_x(j, width):
        block = jnp.dot(a[span(j, width), :], st[0], preferred_element_type=F32)
        ps[j, pl.ds(0, width), :] = block[:, 128:].astype(BF16)
        pcopy(j, width).start()
        keep[lax.rem(j, 2), pl.ds(0, width), :] = block[:, :128]

    def combine_x(j, width):
        pcopy(j, width).wait_recv()
        total = keep[lax.rem(j, 2), pl.ds(0, width), :] + pr[j, pl.ds(0, width), :].astype(F32)
        xs[j, pl.ds(0, width), :] = total.astype(BF16)
        xcopy(j, width).start()

    multiply_x(0, CB)

    @pl.loop(1, FULL)
    def _(j):
        multiply_x(j, CB)
        combine_x(j - 1, CB)

    if TAIL:
        multiply_x(FULL, TAIL)
    combine_x(FULL - 1, CB)
    if TAIL:
        combine_x(FULL, TAIL)

    def second_step(t):
        @pl.when(t < 2 * NB)
        def _():
            second_p(t).wait_recv()
            p2[t] = p2[t] + z2p[t]
            second_t(t).start()

        @pl.when(t >= 1)
        def _():
            k = t - 1
            second_t(k).wait_recv()
            total = p2[k] + z2t[k]
            st_at(k)[...] = total.T.astype(BF16)
            second_s(k).start()

    @pl.when(inner)
    def _():
        @pl.loop(0, NB + 1)
        def _(t):
            second_step(t)

    @pl.when(outer)
    def _():
        @pl.loop(0, NB)
        def _(k):
            second_s(k).wait_recv()

    def multiply_q(j, width):
        block = jnp.dot(a[span(j, width), :], st[1, :, pl.ds(128, 128)], preferred_element_type=F32)
        qs[j, pl.ds(0, width), :] = block.astype(BF16)
        qcopy(j, width).start()

    within = min(FULL // 2, NB)

    @pl.loop(0, FULL)
    def _(j):
        multiply_q(j, CB)

        @pl.when(jnp.logical_and(inner, jnp.logical_and(lax.rem(j, 2) == 1, j // 2 < within)))
        def _():
            second_step(NB + 1 + j // 2)

    if TAIL:
        multiply_q(FULL, TAIL)

    @pl.when(inner)
    def _():
        @pl.loop(NB + 1 + within, 2 * NB + 1)
        def _(t):
            second_step(t)

    @pl.when(outer)
    def _():
        @pl.loop(NB, 2 * NB)
        def _(k):
            second_s(k).wait_recv()

    near = jnp.where(z // 2 == x, 1, 0)
    at = pl.multiple_of(jnp.where(z % 2 == c, 0, 128), 128)
    cols = st[near, :, pl.ds(at, 128)]
    for half in range(2):
        both = lax.dot_general(st[half], cols, (((0,), (0,)), ((), ())), preferred_element_type=F32)
        cpart[half, 0] = both[:128]
        cpart[half, 1] = both[128:]

    def cpair(half):
        return rcopy(cpart.at[half, 1], cpr.at[half], csem.at[half], crem.at[half], {"dp": pair})

    cpair(0).start()
    cpair(1).start()
    cross = rcopy(cxs, cxr, csem.at[2], crem.at[2], {"dp": across})

    def ccopy(k):
        return rcopy(cout.at[0], cout.at[k], csem.at[2 + k], crem.at[2 + k], {"feat": lax.rem(z + k, 4)})

    def finish(j, width):
        total = jnp.dot(a[span(j, width), :], st[1, :, pl.ds(0, 128)], preferred_element_type=F32)
        qcopy(j, width).wait_recv()
        total = total + qr[j, pl.ds(0, width), :].astype(F32)
        xcopy(j, width).wait_recv()
        range_ref[span(j, width), :] = total + xr[j, pl.ds(0, width), :].astype(F32)

    @pl.loop(0, FULL)
    def _(j):
        @pl.when(j == 2)
        def _():
            cpair(0).wait_recv()
            cxs[...] = cpart[0, 0] + cpr[0]
            cross.start()

        finish(j, CB)

    cpair(1).wait_recv()
    cross.wait_recv()
    cout[0] = (cpart[1, 0] + cpr[1] + cxr[...]) * inv_core
    for k in range(1, 4):
        ccopy(k).start()
    if TAIL:
        finish(FULL, TAIL)

    for k in range(1, 4):
        ccopy(k).wait_recv()
    for k in range(4):
        at = pl.multiple_of(lax.rem(z - k + 4, 4) * 128, 128)
        core_ref[:, pl.ds(at, 128)] = cout[k]

    cpair(0).wait_send()
    cpair(1).wait_send()
    cross.wait_send()
    for k in range(1, 4):
        ccopy(k).wait_send()

    @pl.loop(0, NB)
    def _(s):
        @pl.when(outer)
        def _():
            for u in range(2):
                first_p(s, u).wait_send()
                second_p(NB * u + s).wait_send()

        @pl.when(inner)
        def _():
            for u in range(2):
                first_t(s, u).wait_send()
                first_s(s, u).wait_send()
                second_t(NB * u + s).wait_send()
                second_s(NB * u + s).wait_send()

    def drain(j, width):
        pcopy(j, width).wait_send()
        qcopy(j, width).wait_send()
        xcopy(j, width).wait_send()

    @pl.loop(0, FULL)
    def _(j):
        drain(j, CB)

    if TAIL:
        drain(FULL, TAIL)


def fused(activations, test_matrix):
    T, W = activations.shape
    R = test_matrix.shape[1]
    NB = T // TB
    NC = -(-W // CB)
    tokens = T * lax.axis_size("dp")
    units = W * lax.axis_size("feat")
    DMA = pltpu.SemaphoreType.DMA
    V = pltpu.VMEM
    by_unit, core = pl.pallas_call(
        functools.partial(kernel, 1.0 / tokens / units),
        out_shape=(
            jax.ShapeDtypeStruct((W, R // 4), F32),
            jax.ShapeDtypeStruct((R // 4, R), F32),
        ),
        in_specs=[pl.BlockSpec(memory_space=pl.ANY)] * 2,
        out_specs=(pl.BlockSpec(memory_space=pltpu.VMEM),) * 2,
        scratch_shapes=[
            V((W, T), BF16), V((W, 256), BF16), V((2, 256, W), BF16), V((2, T, 256), BF16),
            V((NB, 256, TB), F32), V((2 * NB, 128, TB), F32),
            V((NB, 256, TB), BF16), V((NB, 256, TB), BF16), V((NB, 256, TB), BF16),
            V((2 * NB, 128, TB), F32), V((2 * NB, 128, TB), F32),
            V((NC, CB, 128), BF16), V((NC, CB, 128), BF16), V((NC, CB, 128), BF16), V((NC, CB, 128), BF16),
            V((2, CB, 128), F32),
            V((NC, CB, 128), BF16), V((NC, CB, 128), BF16),
            V((2, 2, 128, 128), F32), V((2, 128, 128), F32), V((128, 128), F32), V((128, 128), F32),
            V((4, 128, 128), F32),
            DMA((NB,)), DMA((2, 2)),
            DMA((2, 2 * NB)), DMA((2, 2 * NB)), DMA((2, 2 * NB)), DMA((2, 2 * NB)), DMA((2, 2 * NB)), DMA((2, 2 * NB)),
            DMA((NC,)), DMA((NC,)), DMA((NC,)), DMA((NC,)), DMA((NC,)), DMA((NC,)),
            DMA((6,)), DMA((6,)),
        ],
        compiler_params=pltpu.CompilerParams(
            collective_id=0, has_side_effects=True, vmem_limit_bytes=63 * 1024 * 1024
        ),
        cost_estimate=pl.CostEstimate(
            flops=4 * T * W * R, bytes_accessed=2 * T * W + 4 * W * R, transcendentals=0
        ),
    )(activations.T, test_matrix)
    return by_unit.T * (1.0 / tokens), core


def solution(mesh):
    placed = (P(("groups", "dp"), "feat"), P("feat", None))

    def body(activations, test_matrix):
        T, W = activations.shape
        fits = (
            mesh.shape["feat"] == 4
            and mesh.shape["dp"] == 4
            and test_matrix.shape[1] == 512
            and T % TB == 0
            and W % 16 == 0
            and 2 * CB <= W <= 7424
            and T <= 1536
        )
        return (fused if fits else plain)(activations, test_matrix)

    return jax.shard_map(
        body,
        mesh=mesh,
        in_specs=placed,
        out_specs=(P(("groups", "dp"), "feat"), P(("groups", "dp"), None)),
        check_vma=False,
    )
```

time: 316 us -> 116 us (0.37)
  waiting for transfers between devices: 251 us -> 0 us
  Pallas kernels: 0 us -> 110 us
  matrix products: 47.3 us -> 0 us
  between operations: 13.8 us -> 0.65 us
    reduce_scatter x2 -> x0, waiting for transfers between devices: 177 us -> none  [the longest x1 114 us: body(): lax.psum_scatter(product * inverse_tokens, 'dp', scatter_dimension=0, til...]
    pallas_call x0 -> x1, Pallas kernels: none -> 110 us  [fused(): pl.pallas_call(functools.partial(kernel, 1.0 / tokens / units), out_shape...]
    dot_general x3 -> x0, matrix products: 47.3 us -> none  [the longest x1 19.9 us: body(): lax.dot_general(sketched, activations, (((0,), (0,)), ((), ())), preferre...]
    all_gather x1 -> x0, waiting for transfers between devices: 37.9 us -> none  [body(): sketched = lax.all_gather(shares, 'feat', axis=1, tiled=True)]
    psum x1 -> x0, waiting for transfers between devices: 35.5 us -> none  [body(): core = lax.psum(core_part, 'feat')]
    mul x0 -> x1, other arithmetic: none -> 4.31 us  [fused(): return (by_unit.T * (1.0 / tokens), core)]
  transfers between devices with their start and end apart: 4 -> 0, of which waited for: 4 -> 0; matrix products, arithmetic and copies ran while one was open for 0% -> 0% of each run, Pallas kernels for 0% -> 0%
where the time goes in v2:
time: 116 us; the launch traced here: 115 us
  Pallas kernels  110 us (95%)
  other arithmetic  4.31 us (4%)
    pallas_call x1, Pallas kernels, fused(): pl.pallas_call(functools.partial(kernel, 1.0 / tokens / units), out_shape...  110 us
    mul x1, other arithmetic, fused(): return (by_unit.T * (1.0 / tokens), core)  4.31 us

profile of v2, /device:TPU:0, one launch (start us, length us, event | category | flops | bytes accessed | tf_op | source)
XLA Modules:
  0.0 115.4 jit_solution(6812643184418545426)
XLA Ops:
  0.6 109.8 %shard_map.41 = (f32[7392,128]{1,0:T(8,128)}, f32[128,512]{1,0:T(8,128)}) custom-call(bf16[7392,1536]{1,0:T(8,128)(2,1)} %bitcast.3, bf16[7392,512]{1,0:T(8,128)(2,1)} %om_hbm.1), custom_call_target="tpu_custom_call" | custom-call | flops 23253221376 | bytes 37847040 | tf_op jit(solution)/shard_map/pallas_call | solution.py:388
  110.4 0.0 copy-start
  110.4 4.3 %multiply_bitcast_fusion = f32[128,7392]{0,1:T(8,128)} fusion(f32[7392,128]{1,0:T(8,128)} %get-tuple-element.4), kind=kLoop, calls=%fused_computation | loop fusion | flops 946176 | bytes 7569408 | tf_op jit(solution)/shard_map/mul | solution.py:418
  114.7 0.0 copy-done
  114.7 0.7 copy.5
Async XLA Ops:
  110.4 4.3 %copy-start = (f32[128,512]{1,0:T(8,128)S(1)}, f32[128,512]{1,0:T(8,128)}, u32[]{:S(2)}) copy-start(f32[128,512]{1,0:T(8,128)} %get-tuple-element.9) | copy-start | bytes 786436
